TPU v7x, 32 devices: a whole 2x2x4 slice. The times are simulated.
32 devices in a mesh: section: 4 (over y, x), tp: 2 (over core), dp: 4 (over z).
Axes of the slice: x: 2, y: 2, z: 4, core: 2. Of those that a mesh axis runs over, the one named last changes fastest.
Arguments:
- hidden_states: bfloat16 [672, 8192], P(None, 'dp'), may hold values from -120 to 120
- norm_gain: float32 [8192], P('dp'), may hold values from 0.5 to 1.5
- lm_head: bfloat16 [8192, 19008], P('dp', ('section', 'tp')), may hold values from -6 to 6
- target_ids: int32 [672], replicated, may hold values from 0 to 19007
Outputs:
- logprobs: bfloat16 [672, 19008], P(None, ('section', 'tp', 'dp'))
- target_logprob: float32 [672], P('dp')
All inputs are finite; a program needn't handle non-finite values.
Results may differ from a plain program's by a relative error of at most 0.0031.
Values may be sent and summed in bfloat16 or wider, within the bound.
A program may use at most 128 MiB of HBM per device.

v0:
```python
import functools

import jax
import jax.numpy as jnp
from jax import lax
from jax.experimental import pallas as pl
from jax.experimental.pallas import tpu as pltpu
from jax.sharding import PartitionSpec as P

D = 8192

epsilon = 1e-06

MESH = pl.DeviceIdType.MESH
CHUNKS = 7
LANES = 128
GRAIN = 8


def to_column(row):
    return jnp.broadcast_to(row, (LANES, row.shape[1])).T[:, :1]


def stack_rows(rows):
    place = lax.broadcasted_iota(jnp.int32, (8, rows[0].shape[1]), 0)
    result = jnp.zeros(place.shape, jnp.float32)
    for index, row in enumerate(rows):
        result = jnp.where(place == index, row, result)
    return result


def columns_to_rows(columns):
    place = lax.broadcasted_iota(jnp.int32, (columns[0].shape[0], LANES), 1)
    result = jnp.zeros(place.shape, jnp.float32)
    for index, column in enumerate(columns):
        result = jnp.where(place == index, column, result)
    return result.T[:8]


def merge(stats):
    tops, totals, picked = stats[:, 0:1], stats[:, 1:2], stats[:, 2:3]
    top = jnp.max(tops, axis=0)
    total = jnp.sum(totals * jnp.exp(tops - top[None]), axis=0)
    return top, total, jnp.sum(picked, axis=0)


def plan(n, width, block):
    origin = block - whole_tiles(block - width)
    starts = [(width * b - origin) // LANES * LANES for b in range(1, n)] + [block - origin]
    right = [None] + [(origin + lo, hi - lo) for lo, hi in zip(starts, starts[1:])]
    ends = [0] + [-(-width * (b + 1) // LANES) * LANES for b in range(n - 1)]
    left = [(lo, hi - lo) for lo, hi in zip(ends, ends[1:])]
    widest = max(piece[1] for piece in right[1:] + left)
    own = [(min(width * b // GRAIN * GRAIN, block - widest), widest) for b in range(n)]
    return right, left, own


def travel_order(n, at):
    going = [(at + n - 1 - b, "right", b) for b in range(n - 1, at, -1)]
    going += [(n - 1 - at + b, "left", b) for b in range(at)]
    return [entry[1:] for entry in sorted(going, key=lambda entry: entry[0])]


def whole_tiles(count):
    return -(-count // LANES) * LANES


def kernel(
    n, tp_size, plane, width,
    x_hbm, w_hbm, gain_ref, target_ref,
    out_ref, target_out_ref,
    x_buf, w_buf, xg, part, final, target_col, target_row,
    squares, all_squares, own_stats, plane_stats, own_merged, line_stats,
    load_sem, send_sem, left_sem, right_sem,
    sq_send, sq_recv, st_send, st_recv, ln_send, ln_recv,
    *travel,
):
    z = lax.axis_index("dp")
    me = lax.axis_index("section") * tp_size + lax.axis_index("tp")
    rc, widest = xg.shape[0] // CHUNKS, part.shape[2]
    right, left, own = plan(n, width, w_buf.shape[0])
    send_right, travel = (None,) + travel[:n - 1], travel[n - 1:]
    from_left, travel = (None,) + travel[:n - 1], travel[n - 1:]
    send_left, from_right = travel[:n - 1], travel[n - 1:]

    load_x = pltpu.make_async_copy(x_hbm, x_buf, load_sem.at[0])
    load_w = pltpu.make_async_copy(w_hbm, w_buf, load_sem.at[1])
    load_x.start()
    load_w.start()

    def plane_peer(step):
        q = lax.rem(me + step, plane)
        return q, {"section": q // tp_size, "tp": lax.rem(q, tp_size)}

    def line_peer(step):
        q = lax.rem(z + step, n)
        return q, {"dp": q}

    barrier = pltpu.get_barrier_semaphore()

    def greet(peer, step, carry):
        pl.semaphore_signal(barrier, inc=1, device_id=peer(step)[1], device_id_type=MESH)
        return carry

    lax.fori_loop(1, plane, functools.partial(greet, plane_peer), 0)
    lax.fori_loop(1, n, functools.partial(greet, line_peer), 0)

    target_col[...] = jnp.broadcast_to(
        target_ref[...].reshape(1, target_ref.shape[0]), (LANES, target_ref.shape[0])
    ).T
    load_x.wait()
    gain = gain_ref[...]

    def prepare(r, carry):
        x = x_buf[pl.ds(pl.multiple_of(r * rc, 16), rc), :].astype(jnp.float32)
        xg[pl.ds(pl.multiple_of(r * rc, 16), rc), :] = (x * gain).astype(jnp.bfloat16)
        squares[r] = columns_to_rows([jnp.sum(x * x, axis=1, keepdims=True)])
        return carry

    lax.fori_loop(0, CHUNKS, prepare, 0)
    pl.semaphore_wait(barrier, plane - 1 + n - 1)

    def squares_copy(step, arriving):
        q, where = line_peer(step)
        slot = q if arriving else z
        return pltpu.make_async_remote_copy(
            src_ref=squares, dst_ref=all_squares.at[slot],
            send_sem=sq_send.at[step], recv_sem=sq_recv.at[slot],
            device_id=where, device_id_type=MESH,
        )

    def stats_copy(r, step, arriving):
        q, where = plane_peer(step)
        slot = q if arriving else me
        return pltpu.make_async_remote_copy(
            src_ref=own_stats.at[r], dst_ref=plane_stats.at[r, slot],
            send_sem=st_send.at[r, step], recv_sem=st_recv.at[r, slot],
            device_id=where, device_id_type=MESH,
        )

    def line_copy(r, step, arriving):
        q, where = line_peer(step)
        slot = q if arriving else z
        return pltpu.make_async_remote_copy(
            src_ref=own_merged.at[r], dst_ref=line_stats.at[r, slot],
            send_sem=ln_send.at[r, step], recv_sem=ln_recv.at[r, slot],
            device_id=where, device_id_type=MESH,
        )

    def each(first, last, action):
        def step_body(step, carry):
            action(step)
            return carry
        lax.fori_loop(first, last, step_body, 0)

    each(1, n, lambda step: squares_copy(step, False).start())
    all_squares[z] = squares[...]
    load_w.wait()

    def right_copy(at, b, r):
        return pltpu.make_async_remote_copy(
            src_ref=send_right[b].at[r], dst_ref=from_left[b].at[r],
            send_sem=send_sem.at[b, r], recv_sem=left_sem.at[b, r],
            device_id={"dp": min(at + 1, n - 1)}, device_id_type=MESH,
        )

    def left_copy(at, b, r):
        return pltpu.make_async_remote_copy(
            src_ref=send_left[b].at[r], dst_ref=from_right[b].at[r],
            send_sem=send_sem.at[b, r], recv_sem=right_sem.at[b, r],
            device_id={"dp": max(at - 1, 0)}, device_id_type=MESH,
        )

    orders = [travel_order(n, at) for at in range(n)]

    def rows_of(r):
        return pl.ds(pl.multiple_of(r * rc, 16), rc)

    def start_own(at, k, r):
        way, b = orders[at][k]
        if way == "right":
            send_right[b][r] = part[k, rows_of(r), :right[b][1]].astype(jnp.bfloat16)
            right_copy(at, b, r).start()
        else:
            send_left[b][r] = part[k, rows_of(r), :left[b][1]].astype(jnp.bfloat16)
            left_copy(at, b, r).start()

    def multiply(k, carry):
        first = 0
        for at in range(n):
            pieces = [(right if way == "right" else left)[b] for way, b in orders[at]] + [own[at]]
            for index, piece in enumerate(pieces):
                first = jnp.where((z == at) & (k == index), piece[0], first)
        part[k] = lax.dot_general(
            xg[...], w_buf[pl.ds(pl.multiple_of(first, GRAIN), widest), :],
            (((1,), (1,)), ((), ())), preferred_element_type=jnp.float32,
        )
        for at in (0, n - 1):
            for index in range(n - 1):
                pl.when((z == at) & (k == index))(functools.partial(start_own, at, index, 0))
        return carry

    lax.fori_loop(0, n, multiply, 0)

    def shifted(parts, lead):
        lanes = jnp.concatenate([p.astype(jnp.float32) for p in parts], axis=1) if len(parts) > 1 else parts[0].astype(jnp.float32)
        if lead:
            lanes = pltpu.roll(lanes, lanes.shape[1] - lead, 1)
        return lanes[:, :final.shape[2]]

    def window(buffers, pieces, origin, at, r):
        lo, hi = width * at, width * (at + 1)
        first, parts = None, []
        for buffer, piece in zip(buffers, pieces):
            if piece is None or piece[0] + piece[1] <= lo or piece[0] >= hi:
                continue
            begin = max(lo - piece[0], 0) // LANES * LANES
            end = min(whole_tiles(hi - piece[0]), whole_tiles(piece[1]))
            if first is None:
                first = piece[0] + begin
            parts.append(buffer[r, :, begin:end])
        return shifted(parts, lo - first)

    def run(at):
        going = orders[at]
        end = at in (0, n - 1)

        def forward(r):
            for k, (way, b) in enumerate(going):
                if way == "right":
                    count = right[b][1]
                    right_copy(at, b, r).wait_recv()
                    send_right[b][r] = (
                        part[k, rows_of(r), :count] + from_left[b][r].astype(jnp.float32)
                    ).astype(jnp.bfloat16)
                    right_copy(at, b, r).start()
                else:
                    count = left[b][1]
                    left_copy(at, b, r).wait_recv()
                    send_left[b][r] = (
                        part[k, rows_of(r), :count] + from_right[b][r].astype(jnp.float32)
                    ).astype(jnp.bfloat16)
                    left_copy(at, b, r).start()

        def finish_sum(r):
            total = jnp.sum(all_squares[:, r], axis=0)[0:1]
            scale = to_column(lax.rsqrt(total / D + epsilon))
            logits = shifted([part[n - 1, rows_of(r)]], width * at - own[at][0])
            if at > 0:
                right_copy(at, at, r).wait_recv()
                logits += window(from_left, right, right[1][0], at, r)
            if at < n - 1:
                left_copy(at, at, r).wait_recv()
                logits += window(from_right, left, 0, at, r)
            logits *= scale
            final[r] = logits
            column = lax.broadcasted_iota(jnp.int32, logits.shape, 1)
            inside = column < width
            top = jnp.max(jnp.where(inside, logits, -jnp.inf), axis=1, keepdims=True)
            sum_exp = jnp.sum(jnp.where(inside, jnp.exp(logits - top), 0.0), axis=1, keepdims=True)
            wanted = target_col[pl.ds(pl.multiple_of(r * rc, 16), rc), 0:1] - (me * n + at) * width
            hit = inside & (column == wanted)
            picked = jnp.sum(jnp.where(hit, logits, 0.0), axis=1, keepdims=True)
            stats = columns_to_rows([top, sum_exp, picked])
            own_stats[r] = stats
            plane_stats[r, me] = stats
            each(1, plane, lambda step: stats_copy(r, step, False).start())

        def merge_plane(r):
            each(1, plane, lambda step: stats_copy(r, step, True).wait_recv())
            merged = stack_rows(merge(plane_stats[r]))
            own_merged[r] = merged
            line_stats[r, at] = merged
            each(1, n, lambda step: line_copy(r, step, False).start())

        def emit(r):
            each(1, n, lambda step: line_copy(r, step, True).wait_recv())
            top, total, picked = merge(line_stats[r])
            rest = jnp.log(total)
            target_row[r, :, :rc] = jnp.broadcast_to(picked - top - rest, (8, rc))
            logprobs = final[r] - to_column(top + rest)
            out_ref[pl.ds(pl.multiple_of(r * rc, 16), rc), :] = logprobs[:, :width].astype(jnp.bfloat16)

        each(1, n, lambda step: squares_copy(step, True).wait_recv())

        def chunk(r, carry):
            if end:
                @pl.when(r + 1 < CHUNKS)
                def _():
                    for k in range(n - 1):
                        start_own(at, k, r + 1)
            else:
                forward(r)

            @pl.when(r >= 1)
            def _():
                merge_plane(r - 1)

            @pl.when(r >= 2)
            def _():
                emit(r - 2)
            finish_sum(r)
            return carry

        lax.fori_loop(0, CHUNKS, chunk, 0)
        merge_plane(CHUNKS - 1)
        emit(CHUNKS - 2)
        emit(CHUNKS - 1)

        own_rows = target_out_ref.shape[1]
        lo = own_rows * at
        lanes = target_row.shape[2]
        place = lax.broadcasted_iota(jnp.int32, (8, lanes), 1) + lo
        row = jnp.zeros((8, lanes), jnp.float32)
        for c in range(lo // rc, (lo + own_rows - 1) // rc + 1):
            moved = pltpu.roll(target_row[c], (c * rc - lo) % lanes, 1)
            row = jnp.where((place >= c * rc) & (place < (c + 1) * rc), moved, row)
        target_out_ref[...] = row[0:1, :own_rows]

        for r in range(CHUNKS):
            for way, b in going:
                (right_copy if way == "right" else left_copy)(at, b, r).wait_send()

    for at in range(n):
        pl.when(z == at)(functools.partial(run, at))

    each(1, n, lambda step: squares_copy(step, False).wait_send())

    def drain(r, carry):
        each(1, plane, lambda step: stats_copy(r, step, False).wait_send())
        each(1, n, lambda step: line_copy(r, step, False).wait_send())
        return carry

    lax.fori_loop(0, CHUNKS, drain, 0)


def body(hidden_states, norm_gain, lm_head, target_ids):
    rows, depth = hidden_states.shape
    block = lm_head.shape[1]
    n, tp_size = lax.axis_size("dp"), lax.axis_size("tp")
    plane = lax.axis_size("section") * tp_size
    width = block // n
    right, left, own = plan(n, width, block)
    widest = max(whole_tiles(piece[1]) for piece in right[1:] + left + own)
    rc = rows // CHUNKS
    own_rows = rows // n
    f32, bf16 = jnp.float32, jnp.bfloat16
    any_space = pl.BlockSpec(memory_space=pl.ANY)
    vmem = pl.BlockSpec(memory_space=pltpu.VMEM)
    dma = pltpu.SemaphoreType.DMA
    travel = [pltpu.VMEM((CHUNKS, rc, whole_tiles(piece[1])), bf16) for piece in right[1:] * 2 + left * 2]
    logprobs, target = pl.pallas_call(
        functools.partial(kernel, n, tp_size, plane, width),
        out_shape=(
            jax.ShapeDtypeStruct((rows, width), bf16),
            jax.ShapeDtypeStruct((1, own_rows), f32),
        ),
        in_specs=[any_space, any_space, vmem, vmem],
        out_specs=(vmem, vmem),
        scratch_shapes=[
            pltpu.VMEM((rows, depth), bf16),
            pltpu.VMEM((block, depth), bf16),
            pltpu.VMEM((rows, depth), bf16),
            pltpu.VMEM((n, rows, widest), f32),
            pltpu.VMEM((CHUNKS, rc, whole_tiles(width)), f32),
            pltpu.VMEM((rows, LANES), jnp.int32),
            pltpu.VMEM((CHUNKS, 8, whole_tiles(rc + own_rows)), f32),
            pltpu.VMEM((CHUNKS, 8, rc), f32),
            pltpu.VMEM((n, CHUNKS, 8, rc), f32),
            pltpu.VMEM((CHUNKS, 8, rc), f32),
            pltpu.VMEM((CHUNKS, plane, 8, rc), f32),
            pltpu.VMEM((CHUNKS, 8, rc), f32),
            pltpu.VMEM((CHUNKS, n, 8, rc), f32),
            dma((2,)),
            dma((n, CHUNKS)),
            dma((n, CHUNKS)),
            dma((n, CHUNKS)),
            dma((n,)),
            dma((n,)),
            dma((CHUNKS, plane)),
            dma((CHUNKS, plane)),
            dma((CHUNKS, n)),
            dma((CHUNKS, n)),
        ] + travel,
        compiler_params=pltpu.CompilerParams(
            collective_id=0, has_side_effects=True, vmem_limit_bytes=52 * 1024 * 1024
        ),
        cost_estimate=pl.CostEstimate(
            flops=2 * rows * depth * block,
            bytes_accessed=2 * (rows * depth + depth * block + rows * width),
            transcendentals=rows * width,
        ),
    )(hidden_states, lm_head.T, norm_gain[None, :], target_ids)
    return logprobs, target.reshape(own_rows)


def solution(mesh):
    placed = (P(None, "dp"), P("dp"), P("dp", ("section", "tp")), P())
    return jax.shard_map(
        body,
        mesh=mesh,
        in_specs=placed,
        out_specs=(P(None, ("section", "tp", "dp")), P("dp")),
        check_vma=False,
    )
```

profile of v0, /device:TPU:0, one launch (start us, length us, event | category | flops | bytes accessed | tf_op | source)
XLA Modules:
  0.0 90.3 jit_solution(6435849600612039526)
XLA Ops:
  0.6 0.0 copy-start
  0.6 0.7 copy-done
  1.3 0.0 copy-start.1
  1.3 0.7 copy-done.1
  2.0 86.8 %shard_map.59 = (bf16[672,594]{1,0:T(8,128)(2,1)S(1)}, f32[1,168]{1,0:T(1,128)S(1)}) custom-call(bf16[672,2048]{1,0:T(8,128)(2,1)} %x_hbm.1, bf16[2376,2048]{1,0:T(8,128)(2,1)} %bitcast.5, f32[1,2048]{1,0:T(1,128)S(1)} %bitcast.4, s32[672]{0:T(1024)S(1)} %copy-done.1), custom_call_target="tpu_custom_call" | custom-call | flops 6539968512 | bytes 13282944 | tf_op jit(solution)/shard_map/pallas_call | solution.py:352
  88.9 0.9 %copy.8 = bf16[672,594]{1,0:T(8,128)(2,1)} copy(bf16[672,594]{1,0:T(8,128)(2,1)S(1)} %get-tuple-element.8) | data formatting | bytes 1596672
  89.8 0.6 copy.9
Async XLA Ops:
  0.6 0.7 copy-start
  1.3 0.7 copy-start.1
where the time goes:
time: 90.6 us; the launch traced here: 90.3 us
  Pallas kernels  86.8 us (96%)
  local copies, waits for them, and re-layouts  2.85 us (3%)
    pallas_call x1, Pallas kernels, body(): pl.pallas_call(functools.partial(kernel, n, tp_size, plane, width), out_s...  86.8 us
    unnamed x6, local copies, waits for them, and re-layouts  2.85 us

commit v1 on v0

--- a/solution.py
+++ b/solution.py
@@ -12,7 +12,7 @@
 epsilon = 1e-06
 
 MESH = pl.DeviceIdType.MESH
-CHUNKS = 7
+CHUNKS = 3
 LANES = 128
 GRAIN = 8
 
@@ -185,22 +185,20 @@
             send_left[b][r] = part[k, rows_of(r), :left[b][1]].astype(jnp.bfloat16)
             left_copy(at, b, r).start()
 
-    def multiply(k, carry):
+    def multiply(r, k, carry):
         first = 0
         for at in range(n):
             pieces = [(right if way == "right" else left)[b] for way, b in orders[at]] + [own[at]]
             for index, piece in enumerate(pieces):
                 first = jnp.where((z == at) & (k == index), piece[0], first)
-        part[k] = lax.dot_general(
-            xg[...], w_buf[pl.ds(pl.multiple_of(first, GRAIN), widest), :],
+        part[k, rows_of(r), :] = lax.dot_general(
+            xg[rows_of(r), :], w_buf[pl.ds(pl.multiple_of(first, GRAIN), widest), :],
             (((1,), (1,)), ((), ())), preferred_element_type=jnp.float32,
         )
         for at in (0, n - 1):
             for index in range(n - 1):
-                pl.when((z == at) & (k == index))(functools.partial(start_own, at, index, 0))
+                pl.when((z == at) & (k == index))(functools.partial(start_own, at, index, r))
         return carry
-
-    lax.fori_loop(0, n, multiply, 0)
 
     def shifted(parts, lead):
         lanes = jnp.concatenate([p.astype(jnp.float32) for p in parts], axis=1) if len(parts) > 1 else parts[0].astype(jnp.float32)
@@ -221,7 +219,7 @@
             parts.append(buffer[r, :, begin:end])
         return shifted(parts, lo - first)
 
-    def run(at):
+    def run(at, stage, stage_r):
         going = orders[at]
         end = at in (0, n - 1)
 
@@ -281,31 +279,26 @@
             logprobs = final[r] - to_column(top + rest)
             out_ref[pl.ds(pl.multiple_of(r * rc, 16), rc), :] = logprobs[:, :width].astype(jnp.bfloat16)
 
-        each(1, n, lambda step: squares_copy(step, True).wait_recv())
-
-        def chunk(r, carry):
-            if end:
-                @pl.when(r + 1 < CHUNKS)
-                def _():
-                    for k in range(n - 1):
-                        start_own(at, k, r + 1)
+        if stage == "before":
+            if not end:
+                forward(stage_r)
             else:
-                forward(r)
-
-            @pl.when(r >= 1)
-            def _():
-                merge_plane(r - 1)
-
-            @pl.when(r >= 2)
-            def _():
-                emit(r - 2)
-            finish_sum(r)
+                pl.when(stage_r >= 1)(lambda: merge_plane(stage_r - 1))
+            return
+        if stage == "after":
+            if not end:
+                pl.when(stage_r >= 1)(lambda: merge_plane(stage_r - 1))
+            finish_sum(stage_r)
+            return
+
+        emit(0)
+        merge_plane(CHUNKS - 1)
+
+        def emit_step(r, carry):
+            emit(r)
             return carry
 
-        lax.fori_loop(0, CHUNKS, chunk, 0)
-        merge_plane(CHUNKS - 1)
-        emit(CHUNKS - 2)
-        emit(CHUNKS - 1)
+        lax.fori_loop(1, CHUNKS, emit_step, 0)
 
         own_rows = target_out_ref.shape[1]
         lo = own_rows * at
@@ -321,8 +314,26 @@
             for way, b in going:
                 (right_copy if way == "right" else left_copy)(at, b, r).wait_send()
 
-    for at in range(n):
-        pl.when(z == at)(functools.partial(run, at))
+    def run_here(stage, r):
+        for at in range(n):
+            pl.when(z == at)(functools.partial(run, at, stage, r))
+
+    def chunk(t, carry):
+        pl.when(t >= 1)(lambda: run_here("before", t - 1))
+
+        @pl.when(t < CHUNKS)
+        def _():
+            lax.fori_loop(0, n, functools.partial(multiply, t), 0)
+
+        @pl.when(t == 0)
+        def _():
+            each(1, n, lambda step: squares_copy(step, True).wait_recv())
+
+        pl.when(t >= 1)(lambda: run_here("after", t - 1))
+        return carry
+
+    lax.fori_loop(0, CHUNKS + 1, chunk, 0)
+    run_here("last", 0)
 
     each(1, n, lambda step: squares_copy(step, False).wait_send())
 

time: 90.6 us -> 78.2 us (0.86)
  Pallas kernels: 86.8 us -> 74.5 us
    pallas_call x1, Pallas kernels: 86.8 us -> 74.5 us  [body(): pl.pallas_call(functools.partial(kernel, n, tp_size, plane, width), out_s...]
where the time goes in v1:
time: 78.2 us; the launch traced here: 78 us
  Pallas kernels  74.5 us (95%)
  local copies, waits for them, and re-layouts  2.85 us (4%)
    pallas_call x1, Pallas kernels, body(): pl.pallas_call(functools.partial(kernel, n, tp_size, plane, width), out_s...  74.5 us
    unnamed x6, local copies, waits for them, and re-layouts  2.85 us

profile of v1, /device:TPU:0, one launch (start us, length us, event | category | flops | bytes accessed | tf_op | source)
XLA Modules:
  0.0 78.0 jit_solution(17209913201281843385)
XLA Ops:
  0.6 0.0 copy-start
  0.6 0.7 copy-done
  1.3 0.0 copy-start.1
  1.3 0.7 copy-done.1
  2.0 74.5 %shard_map.59 = (bf16[672,594]{1,0:T(8,128)(2,1)S(1)}, f32[1,168]{1,0:T(1,128)S(1)}) custom-call(bf16[672,2048]{1,0:T(8,128)(2,1)} %x_hbm.1, bf16[2376,2048]{1,0:T(8,128)(2,1)} %bitcast.5, f32[1,2048]{1,0:T(1,128)S(1)} %bitcast.4, s32[672]{0:T(1024)S(1)} %copy-done.1), custom_call_target="tpu_custom_call" | custom-call | flops 6539968512 | bytes 13282944 | tf_op jit(solution)/shard_map/pallas_call | solution.py:363
  76.5 0.9 %copy.8 = bf16[672,594]{1,0:T(8,128)(2,1)} copy(bf16[672,594]{1,0:T(8,128)(2,1)S(1)} %get-tuple-element.8) | data formatting | bytes 1596672
  77.4 0.6 copy.9
Async XLA Ops:
  0.6 0.7 copy-start
  1.3 0.7 copy-start.1
